TPU v7x, 128 devices: a whole 4x4x4 slice. The times are simulated.
128 devices in a mesh: row: 4 (over y), col: 16 (over x, z_hi, core), depth: 2 (over z_lo).
Axes of the slice: x: 4, y: 4, z: 4 (z_hi: 2, z_lo: 2; z = z_hi * 2 + z_lo), core: 2. Of those that a mesh axis runs over, the one named last changes fastest.
Arguments:
- values: bfloat16 [800, 80, 128, 128], P(('row', 'depth'), 'col'), may hold values from -2 to 2
- pattern: int32 [800, 80], P(('row', 'depth'), 'col'), may hold values from 0 to 49, as said below
- branch_flag: int32 [40], replicated, may hold values from 0 to 1, as said below
Outputs:
- purified: bfloat16 [40, 80, 128, 128], P(('row', 'depth'), 'col')
Inputs may be any that keep to these rules, and one draw needn't show every extreme that they name: `pattern`: block columns fall into classes with 5 members in every column panel; block (i, j) is nonzero exactly when i and j are in the same class, and the 5 slots of a block row in panel c list, in no particular order, the distinct panel-local indices of the members of its class in that panel. `branch_flag`: exactly half of the entries, rounded down, are 1; the rest are 0.
All inputs are finite; a program needn't handle non-finite values.
Results may differ from a plain program's by a relative error of at most 0.001.
Values may be sent and summed in bfloat16 or wider, within the bound.
A program may use at most 128 MiB of HBM per device.

v0:
```python
import jax
import jax.numpy as jnp
from jax import lax
from jax.sharding import PartitionSpec as P

SLAB_DEV = 5


def broadcast(block, axis, holder):
    block = jnp.where(lax.axis_index(axis) == holder, block, jnp.zeros_like(block))
    return lax.psum(block, axis)


def body(values, pattern, branch_flag):
    groups = lax.axis_size(("row", "depth"))
    shard_index = lax.axis_index(("row", "depth"))
    panels = lax.axis_size("col")
    rows_here = values.shape[0]
    slot_count = values.shape[1]
    block_size = values.shape[2]
    total_rows = rows_here * groups
    panel_cols = total_rows // panels
    stride = rows_here // SLAB_DEV
    panel_count = max(1, rows_here // panel_cols)
    first_panel = shard_index * rows_here // panel_cols
    mine_vals = values[::stride]
    mine_cols = pattern[::stride]
    slab_vals, slab_cols = (
        lax.all_gather(mine_vals, ("row", "depth"), axis=0, tiled=True),
        lax.all_gather(mine_cols, ("row", "depth"), axis=0, tiled=True),
    )
    piece_vals = []
    piece_cols = []
    for offset in range(panel_count):
        root_panel = first_panel + offset
        got_vals, got_cols = (
            broadcast(slab_vals, "col", root_panel),
            broadcast(slab_cols, "col", root_panel),
        )
        piece_vals.append(got_vals)
        piece_cols.append(got_cols + root_panel * panel_cols)
    left_vals = jnp.concatenate(piece_vals, 1)
    left_cols = jnp.concatenate(piece_cols, 1)
    slab_total = left_vals.shape[0]
    left_slots = left_vals.shape[1]
    local_rows = left_cols - shard_index * rows_here
    inside = (local_rows >= 0) & (local_rows < rows_here)
    local_rows = jnp.clip(local_rows, 0, rows_here - 1).astype(jnp.int32)
    left_vals = jnp.where(inside[:, :, None, None], left_vals, jnp.zeros((), left_vals.dtype))
    right_cols = pattern[local_rows]
    match = right_cols[:, :, None, :] == slab_cols[:, None, :, None]
    present = jnp.any(match, axis=3)
    slot_iota = lax.broadcasted_iota(jnp.int32, match.shape, 3)
    chosen = jnp.sum(jnp.where(match, slot_iota, 0), axis=3)
    group_rows = slab_total // groups

    def group_product(items):
        block_vals, row_index, slot_index, live = items
        picked = values[row_index[:, :, None], slot_index]
        picked = jnp.where(live[:, :, :, None, None], picked, jnp.zeros((), picked.dtype))
        return jnp.einsum(
            "ilab,ilmbc->imac", block_vals, picked, preferred_element_type=jnp.float32
        )

    partial_terms = lax.map(
        group_product,
        (
            left_vals.reshape(groups, group_rows, left_slots, block_size, block_size),
            local_rows.reshape(groups, group_rows, left_slots),
            chosen.reshape(groups, group_rows, left_slots, slot_count),
            present.reshape(groups, group_rows, left_slots, slot_count),
        ),
    )
    partial_terms = partial_terms.reshape(slab_total, slot_count, block_size, block_size)
    summed = lax.psum_scatter(partial_terms, ("row", "depth"), scatter_dimension=0, tiled=True)
    own_count = mine_vals.shape[0]
    own_flags = lax.dynamic_slice_in_dim(branch_flag, shard_index * own_count, own_count)
    own = mine_vals.astype(jnp.float32)
    result = jnp.where(own_flags[:, None, None, None] == 1, summed, 2.0 * own - summed)
    return result.astype(jnp.bfloat16)


def solution(mesh):
    in_specs = (P(("row", "depth"), "col", None, None), P(("row", "depth"), "col"), P())
    out_specs = P(("row", "depth"), "col", None, None)
    return jax.shard_map(body, mesh=mesh, in_specs=in_specs, out_specs=out_specs, check_vma=False)
```

profile of v0, /device:TPU:1, one launch (start us, length us, event | category | flops | bytes accessed | tf_op | source)
XLA Modules:
  0.0 1057.2 jit_solution(11381887055578751937)
XLA Ops:
  6.5 2.1 slice.7
  8.8 137.5 %all-gather.3.cloned.1.call-done = bf16[40,5,128,128]{3,2,1,0:T(8,128)(2,1)} async-done(((bf16[5,5,128,128]{3,2,1,0:T(8,128)(2,1)}), bf16[40,5,128,128]{3,2,1,0:T(8,128)(2,1)}) %all-gather.3.cloned.1.call-update) | async-done | bytes 6553616 | tf_op jit(solution)/shard_map/all_gather | solution.py:29
  146.2 8.4 broadcast_select_fusion.1
  154.7 0.6 copy-done
  155.4 30.0 %all-gather = s32[8,5,5]{2,1,0:T(8,128)S(1)} all-gather(s32[1,5,5]{2,1,0:T(8,128)S(1)} %bitcast.59), channel_id=1, replica_groups=mesh['row'=4,'col'=16,'depth'=2] {'row','depth'}, dimensions={0}, use_global_device_ids=true | all-gather | bytes 900 | tf_op jit(solution)/shard_map/all_gather | solution.py:30
  185.5 15.9 %all-reduce = (s32[40,5]{0,1:T(8,128)S(1)}, s32[40,5]{0,1:T(8,128)S(1)}) all-reduce(s32[40,5]{0,1:T(8,128)S(1)} %get-tuple-element.92, s32[40,5]{0,1:T(8,128)S(1)} %get-tuple-element.91), channel_id=1, replica_groups=mesh['row'=4,'col'=16,'depth'=2] {'col'}, use_global_device_ids=true, to_apply=%region_1.2 | all-reduce | flops 400 | bytes 3200 | tf_op jit(solution)/shard_map/psum | solution.py:11
  201.6 0.1 copy.51
  202.0 1.1 gather_fusion.1
  203.6 0.9 copy.60
  204.6 0.2 copy.59
  204.9 248.1 %all-reduce.4.cloned.1.call-done = (bf16[8,5,5,128,128]{4,3,2,1,0:T(8,128)(2,1)}, bf16[8,5,5,128,128]{4,3,2,1,0:T(8,128)(2,1)}) async-done(((bf16[8,5,5,128,128]{4,3,2,1,0:T(8,128)(2,1)}, bf16[8,5,5,128,128]{4,3,2,1,0:T(8,128)(2,1)}), (bf16[8,5,5,128,128]{4,3,2,1,0:T(8,128)(2,1)}, bf16[8,5,5,128,128]{4,3,2,1,0:T(8,128)(2,1)})) %all-reduce.4.cloned.1.call-update) | async-done | bytes 13107216 | tf_op jit(solution)/shard_map/psum | solution.py:11
  453.0 10.1 maximum_select_fusion
  463.1 327.5 %while.10 = (s32[]{:T(128)}, f32[8,5,5,128,128]{4,3,2,1,0:T(8,128)}, pred[8,5,10,5]{2,3,1,0:T(8,128)(4,1)S(1)}, s32[8,5,10]{2,1,0:T(8,128)S(1)}, s32[8,5,10,5]{3...) while((s32[]{:T(128)}, ...), condition=%wide.region_7.8_spmd, body=%wide.region_6.7_spmd.sunk | while | flops 1052673728 | bytes 50798872 | solution.py:65
  463.1 0.9 fusion.30
  464.1 17.9 %gather_fusion = bf16[250,128,128]{2,1,0:T(8,128)(2,1)} fusion(bf16[100,5,128,128]{3,2,1,0:T(8,128)(2,1)} %get-tuple-element.159, s32[250]{0:T(256)S(1)} %reshape.163), kind=kCustom, calls=%fused_computation.clone.1 | custom fusion | bytes 16386000 | tf_op jit(solution)/shard_map/while/body/eval_jaxpr/gather | solution.py:59
  482.1 12.8 %copy.65 = bf16[5,10,5,128,128]{3,4,1,2,0:T(8,128)(2,1)} copy(bf16[5,10,5,128,128]{4,3,2,1,0:T(8,128)(2,1)} %bitcast.52) | data formatting | bytes 16384000 | tf_op jit(solution)/shard_map/while/body/eval_jaxpr/gather | solution.py:59
  494.9 6.1 fusion.31
  501.0 1.8 copy.66
  502.8 1.3 constant_dynamic-update-slice_fusion.2
  504.1 0.9 fusion.30
  505.0 17.9 %gather_fusion = bf16[250,128,128]{2,1,0:T(8,128)(2,1)} fusion(bf16[100,5,128,128]{3,2,1,0:T(8,128)(2,1)} %get-tuple-element.159, s32[250]{0:T(256)S(1)} %reshape.163), kind=kCustom, calls=%fused_computation.clone.1 | custom fusion | bytes 16386000 | tf_op jit(solution)/shard_map/while/body/eval_jaxpr/gather | solution.py:59
  523.0 12.8 %copy.65 = bf16[5,10,5,128,128]{3,4,1,2,0:T(8,128)(2,1)} copy(bf16[5,10,5,128,128]{4,3,2,1,0:T(8,128)(2,1)} %bitcast.52) | data formatting | bytes 16384000 | tf_op jit(solution)/shard_map/while/body/eval_jaxpr/gather | solution.py:59
  535.8 6.1 fusion.31
  541.9 1.8 copy.66
  543.7 1.3 constant_dynamic-update-slice_fusion.2
  545.0 0.9 fusion.30
  546.0 17.9 %gather_fusion = bf16[250,128,128]{2,1,0:T(8,128)(2,1)} fusion(bf16[100,5,128,128]{3,2,1,0:T(8,128)(2,1)} %get-tuple-element.159, s32[250]{0:T(256)S(1)} %reshape.163), kind=kCustom, calls=%fused_computation.clone.1 | custom fusion | bytes 16386000 | tf_op jit(solution)/shard_map/while/body/eval_jaxpr/gather | solution.py:59
  563.9 12.8 %copy.65 = bf16[5,10,5,128,128]{3,4,1,2,0:T(8,128)(2,1)} copy(bf16[5,10,5,128,128]{4,3,2,1,0:T(8,128)(2,1)} %bitcast.52) | data formatting | bytes 16384000 | tf_op jit(solution)/shard_map/while/body/eval_jaxpr/gather | solution.py:59
  576.8 6.1 fusion.31
  582.9 1.8 copy.66
  584.6 1.3 constant_dynamic-update-slice_fusion.2
  585.9 0.9 fusion.30
  586.9 17.9 %gather_fusion = bf16[250,128,128]{2,1,0:T(8,128)(2,1)} fusion(bf16[100,5,128,128]{3,2,1,0:T(8,128)(2,1)} %get-tuple-element.159, s32[250]{0:T(256)S(1)} %reshape.163), kind=kCustom, calls=%fused_computation.clone.1 | custom fusion | bytes 16386000 | tf_op jit(solution)/shard_map/while/body/eval_jaxpr/gather | solution.py:59
  604.8 12.8 %copy.65 = bf16[5,10,5,128,128]{3,4,1,2,0:T(8,128)(2,1)} copy(bf16[5,10,5,128,128]{4,3,2,1,0:T(8,128)(2,1)} %bitcast.52) | data formatting | bytes 16384000 | tf_op jit(solution)/shard_map/while/body/eval_jaxpr/gather | solution.py:59
  617.7 6.1 fusion.31
  623.8 1.8 copy.66
  625.6 1.3 constant_dynamic-update-slice_fusion.2
  626.9 0.9 fusion.30
  627.8 17.9 %gather_fusion = bf16[250,128,128]{2,1,0:T(8,128)(2,1)} fusion(bf16[100,5,128,128]{3,2,1,0:T(8,128)(2,1)} %get-tuple-element.159, s32[250]{0:T(256)S(1)} %reshape.163), kind=kCustom, calls=%fused_computation.clone.1 | custom fusion | bytes 16386000 | tf_op jit(solution)/shard_map/while/body/eval_jaxpr/gather | solution.py:59
  645.8 12.8 %copy.65 = bf16[5,10,5,128,128]{3,4,1,2,0:T(8,128)(2,1)} copy(bf16[5,10,5,128,128]{4,3,2,1,0:T(8,128)(2,1)} %bitcast.52) | data formatting | bytes 16384000 | tf_op jit(solution)/shard_map/while/body/eval_jaxpr/gather | solution.py:59
  658.6 6.1 fusion.31
  664.7 1.8 copy.66
  666.5 1.3 constant_dynamic-update-slice_fusion.2
  667.8 0.9 fusion.30
  668.7 17.9 %gather_fusion = bf16[250,128,128]{2,1,0:T(8,128)(2,1)} fusion(bf16[100,5,128,128]{3,2,1,0:T(8,128)(2,1)} %get-tuple-element.159, s32[250]{0:T(256)S(1)} %reshape.163), kind=kCustom, calls=%fused_computation.clone.1 | custom fusion | bytes 16386000 | tf_op jit(solution)/shard_map/while/body/eval_jaxpr/gather | solution.py:59
  686.7 12.8 %copy.65 = bf16[5,10,5,128,128]{3,4,1,2,0:T(8,128)(2,1)} copy(bf16[5,10,5,128,128]{4,3,2,1,0:T(8,128)(2,1)} %bitcast.52) | data formatting | bytes 16384000 | tf_op jit(solution)/shard_map/while/body/eval_jaxpr/gather | solution.py:59
  699.5 6.1 fusion.31
  705.6 1.8 copy.66
  707.4 1.3 constant_dynamic-update-slice_fusion.2
  708.7 0.9 fusion.30
  709.7 17.9 %gather_fusion = bf16[250,128,128]{2,1,0:T(8,128)(2,1)} fusion(bf16[100,5,128,128]{3,2,1,0:T(8,128)(2,1)} %get-tuple-element.159, s32[250]{0:T(256)S(1)} %reshape.163), kind=kCustom, calls=%fused_computation.clone.1 | custom fusion | bytes 16386000 | tf_op jit(solution)/shard_map/while/body/eval_jaxpr/gather | solution.py:59
  727.6 12.8 %copy.65 = bf16[5,10,5,128,128]{3,4,1,2,0:T(8,128)(2,1)} copy(bf16[5,10,5,128,128]{4,3,2,1,0:T(8,128)(2,1)} %bitcast.52) | data formatting | bytes 16384000 | tf_op jit(solution)/shard_map/while/body/eval_jaxpr/gather | solution.py:59
  740.5 6.1 fusion.31
  746.6 1.8 copy.66
  748.3 1.3 constant_dynamic-update-slice_fusion.2
  749.6 0.9 fusion.30
  750.6 17.9 %gather_fusion = bf16[250,128,128]{2,1,0:T(8,128)(2,1)} fusion(bf16[100,5,128,128]{3,2,1,0:T(8,128)(2,1)} %get-tuple-element.159, s32[250]{0:T(256)S(1)} %reshape.163), kind=kCustom, calls=%fused_computation.clone.1 | custom fusion | bytes 16386000 | tf_op jit(solution)/shard_map/while/body/eval_jaxpr/gather | solution.py:59
  768.5 12.8 %copy.65 = bf16[5,10,5,128,128]{3,4,1,2,0:T(8,128)(2,1)} copy(bf16[5,10,5,128,128]{4,3,2,1,0:T(8,128)(2,1)} %bitcast.52) | data formatting | bytes 16384000 | tf_op jit(solution)/shard_map/while/body/eval_jaxpr/gather | solution.py:59
  781.4 6.1 fusion.31
  787.5 1.8 copy.66
  789.3 1.4 constant_dynamic-update-slice_fusion.2
  790.7 0.6 copy-done.1
  791.4 256.4 %reduce-scatter.2.cloned.1.call-done = f32[5,5,128,128]{3,2,1,0:T(8,128)} async-done(((f32[40,5,128,128]{3,2,1,0:T(8,128)}), f32[5,5,128,128]{3,2,1,0:T(8,128)}) %reduce-scatter.2.cloned.1.call-update) | async-done | bytes 1638416 | tf_op jit(solution)/shard_map/reduce_scatter | solution.py:75
  1047.8 2.9 fusion.18
  (54 shorter events, 2.5 us)
Async XLA Ops:
  6.5 139.7 %all-gather.3.cloned.1.call-start = ((), (), s32[]{:S(2)}) async-start(), calls=%async_computation.1 | async-start | bytes 7372800 | tf_op jit(solution)/shard_map/all_gather | solution.py:29
  8.7 444.4 %all-reduce.4.cloned.1.call-start = ((), (), s32[]{:S(2)}) async-start(), calls=%async_computation.3 | async-start | bytes 26214400 | tf_op jit(solution)/shard_map/psum | solution.py:11
  154.6 0.7 copy-start
  154.6 893.1 %reduce-scatter.2.cloned.1.call-start = ((), (), s32[]{:S(2)}) async-start(), calls=%async_computation.2 | async-start | bytes 14745600 | tf_op jit(solution)/shard_map/reduce_scatter | solution.py:75
  790.6 0.7 copy-start.1
Sparse Core Ops, SparseCore 0:
  9.0 137.1 all-gather.2
  154.8 298.2 all-reduce.3
  790.8 256.9 reduce-scatter.1
where the time goes:
time: 1060 us
  waiting for transfers between devices  642 us (61%)
  local copies, waits for them, and re-layouts  278 us (26%)
  matrix products  48.7 us (5%)
  blocking collectives  45.9 us (4%)
  other arithmetic  28.6 us (3%)
  between operations  13.2 us (1%)
    reduce_scatter x1, waiting for transfers between devices, body(): lax.psum_scatter(partial_terms, ('row', 'depth'), scatter_dimension=0, ti...  256 us
    psum x1, waiting for transfers between devices, broadcast(): return lax.psum(block, axis)  248 us
    gather x16, local copies, waits for them, and re-layouts, group_product(): picked = values[row_index[:, :, None], slot_index]  246 us
    all_gather x1, waiting for transfers between devices, body(): lax.all_gather(mine_vals, ('row', 'depth'), axis=0, tiled=True)  137 us
    dot_general x8, matrix products, group_product(): jnp.einsum('ilab,ilmbc->imac', block_vals, picked, preferred_element_type...  48.7 us
    all_gather x1, blocking collectives, body(): lax.all_gather(mine_cols, ('row', 'depth'), axis=0, tiled=True)  30 us
    dynamic_update_slice x16, local copies, waits for them, and re-layouts, body(): lax.map(group_product, (left_vals.reshape(groups, group_rows, left_slots,...  24.6 us
  transfers between devices with their start and end apart: 3, of which 3 were waited for; matrix products, arithmetic and copies ran while one was open for 0% of the time, Pallas kernels for 0%

commit v1 on v0

--- a/solution.py
+++ b/solution.py
@@ -26,7 +26,12 @@
     mine_vals = values[::stride]
     mine_cols = pattern[::stride]
     slab_vals, slab_cols = (
-        lax.all_gather(mine_vals, ("row", "depth"), axis=0, tiled=True),
+        jnp.concatenate(
+            lax.all_to_all(
+                jnp.stack([mine_vals] * lax.axis_size(("row", "depth"))), ("row", "depth"), 0, 0
+            ),
+            axis=0,
+        ),
         lax.all_gather(mine_cols, ("row", "depth"), axis=0, tiled=True),
     )
     piece_vals = []

time: 1060 us -> 1020 us (0.962)
  waiting for transfers between devices: 642 us -> 595 us
    all_gather x1 -> x0, waiting for transfers between devices: 137 us -> none  [body(): lax.all_gather(mine_vals, ('row', 'depth'), axis=0, tiled=True)]
    all_to_all x0 -> x1, waiting for transfers between devices: none -> 90.5 us  [body(): lax.all_to_all(jnp.stack([mine_vals] * lax.axis_size(('row', 'depth'))),...]
where the time goes in v1:
time: 1020 us
  waiting for transfers between devices  595 us (58%)
  local copies, waits for them, and re-layouts  282 us (28%)
  matrix products  48.7 us (5%)
  blocking collectives  44.5 us (4%)
  other arithmetic  28.6 us (3%)
  between operations  13.5 us (1%)
    reduce_scatter x1, waiting for transfers between devices, body(): lax.psum_scatter(partial_terms, ('row', 'depth'), scatter_dimension=0, ti...  256 us
    psum x1, waiting for transfers between devices, broadcast(): return lax.psum(block, axis)  248 us
    gather x16, local copies, waits for them, and re-layouts, group_product(): picked = values[row_index[:, :, None], slot_index]  246 us
    all_to_all x1, waiting for transfers between devices, body(): lax.all_to_all(jnp.stack([mine_vals] * lax.axis_size(('row', 'depth'))),...  90.5 us
    dot_general x8, matrix products, group_product(): jnp.einsum('ilab,ilmbc->imac', block_vals, picked, preferred_element_type...  48.7 us
    all_gather x1, blocking collectives, body(): lax.all_gather(mine_cols, ('row', 'depth'), axis=0, tiled=True)  28.3 us
    dynamic_update_slice x16, local copies, waits for them, and re-layouts, body(): lax.map(group_product, (left_vals.reshape(groups, group_rows, left_slots,...  24.6 us
  transfers between devices with their start and end apart: 3, of which 3 were waited for; matrix products, arithmetic and copies ran while one was open for 0% of the time, Pallas kernels for 0%

profile of v1, /device:TPU:1, one launch (start us, length us, event | category | flops | bytes accessed | tf_op | source)
XLA Modules:
  0.0 1018.7 jit_solution(11538768025000125757)
XLA Ops:
  6.5 1.2 slice.7
  7.8 4.4 stack.2
  12.2 6.4 all-to-all-start
  18.6 90.5 %all-to-all-done = bf16[8,5,5,128,128]{4,3,2,1,0:T(8,128)(2,1)} async-done(((bf16[8,5,5,128,128]{4,3,2,1,0:T(8,128)(2,1)}), bf16[8,5,5,128,128]{4,3,2,1,0:T(8,128)(2,1)}, u32[]{:S(2)}, u32[]{:S(2)}) %all-to-all-start) | async-done | bytes 6553632 | tf_op jit(solution)/shard_map/all_to_all | solution.py:30
  109.1 8.4 broadcast_select_fusion.1
  117.5 0.6 copy-done
  118.3 28.3 %all-gather = s32[8,5,5]{2,1,0:T(8,128)S(1)} all-gather(s32[1,5,5]{2,1,0:T(8,128)S(1)} %bitcast.55), channel_id=1, replica_groups=mesh['row'=4,'col'=16,'depth'=2] {'row','depth'}, dimensions={0}, use_global_device_ids=true | all-gather | bytes 900 | tf_op jit(solution)/shard_map/all_gather | solution.py:35
  146.7 16.2 %all-reduce = (s32[40,5]{0,1:T(8,128)S(1)}, s32[40,5]{0,1:T(8,128)S(1)}) all-reduce(s32[40,5]{0,1:T(8,128)S(1)} %get-tuple-element.92, s32[40,5]{0,1:T(8,128)S(1)} %get-tuple-element.91), channel_id=1, replica_groups=mesh['row'=4,'col'=16,'depth'=2] {'col'}, use_global_device_ids=true, to_apply=%region_1.2 | all-reduce | flops 400 | bytes 3200 | tf_op jit(solution)/shard_map/psum | solution.py:11
  163.4 1.1 gather_fusion.1
  165.0 0.9 copy.60
  166.4 247.9 %all-reduce.4.cloned.1.call-done = (bf16[8,5,5,128,128]{4,3,2,1,0:T(8,128)(2,1)}, bf16[8,5,5,128,128]{4,3,2,1,0:T(8,128)(2,1)}) async-done(((bf16[8,5,5,128,128]{4,3,2,1,0:T(8,128)(2,1)}, bf16[8,5,5,128,128]{4,3,2,1,0:T(8,128)(2,1)}), (bf16[8,5,5,128,128]{4,3,2,1,0:T(8,128)(2,1)}, bf16[8,5,5,128,128]{4,3,2,1,0:T(8,128)(2,1)})) %all-reduce.4.cloned.1.call-update) | async-done | bytes 13107216 | tf_op jit(solution)/shard_map/psum | solution.py:11
  414.2 10.1 maximum_select_fusion
  424.3 327.5 %while.10 = (s32[]{:T(128)}, f32[8,5,5,128,128]{4,3,2,1,0:T(8,128)}, pred[8,5,10,5]{2,3,1,0:T(8,128)(4,1)S(1)}, s32[8,5,10]{2,1,0:T(8,128)S(1)}, s32[8,5,10,5]{3...) while((s32[]{:T(128)}, ...), condition=%wide.region_7.8_spmd, body=%wide.region_6.7_spmd.sunk | while | flops 1052673728 | bytes 50798872 | solution.py:70
  424.3 0.9 fusion.30
  425.3 17.9 %gather_fusion = bf16[250,128,128]{2,1,0:T(8,128)(2,1)} fusion(bf16[100,5,128,128]{3,2,1,0:T(8,128)(2,1)} %get-tuple-element.159, s32[250]{0:T(256)S(1)} %reshape.174), kind=kCustom, calls=%fused_computation.clone.1 | custom fusion | bytes 16386000 | tf_op jit(solution)/shard_map/while/body/eval_jaxpr/gather | solution.py:64
  443.2 12.8 %copy.65 = bf16[5,10,5,128,128]{3,4,1,2,0:T(8,128)(2,1)} copy(bf16[5,10,5,128,128]{4,3,2,1,0:T(8,128)(2,1)} %bitcast.50) | data formatting | bytes 16384000 | tf_op jit(solution)/shard_map/while/body/eval_jaxpr/gather | solution.py:64
  456.1 6.1 fusion.31
  462.2 1.8 copy.66
  464.0 1.3 constant_dynamic-update-slice_fusion.2
  465.2 0.9 fusion.30
  466.2 17.9 %gather_fusion = bf16[250,128,128]{2,1,0:T(8,128)(2,1)} fusion(bf16[100,5,128,128]{3,2,1,0:T(8,128)(2,1)} %get-tuple-element.159, s32[250]{0:T(256)S(1)} %reshape.174), kind=kCustom, calls=%fused_computation.clone.1 | custom fusion | bytes 16386000 | tf_op jit(solution)/shard_map/while/body/eval_jaxpr/gather | solution.py:64
  484.2 12.8 %copy.65 = bf16[5,10,5,128,128]{3,4,1,2,0:T(8,128)(2,1)} copy(bf16[5,10,5,128,128]{4,3,2,1,0:T(8,128)(2,1)} %bitcast.50) | data formatting | bytes 16384000 | tf_op jit(solution)/shard_map/while/body/eval_jaxpr/gather | solution.py:64
  497.0 6.1 fusion.31
  503.1 1.8 copy.66
  504.9 1.3 constant_dynamic-update-slice_fusion.2
  506.2 0.9 fusion.30
  507.2 17.9 %gather_fusion = bf16[250,128,128]{2,1,0:T(8,128)(2,1)} fusion(bf16[100,5,128,128]{3,2,1,0:T(8,128)(2,1)} %get-tuple-element.159, s32[250]{0:T(256)S(1)} %reshape.174), kind=kCustom, calls=%fused_computation.clone.1 | custom fusion | bytes 16386000 | tf_op jit(solution)/shard_map/while/body/eval_jaxpr/gather | solution.py:64
  525.1 12.8 %copy.65 = bf16[5,10,5,128,128]{3,4,1,2,0:T(8,128)(2,1)} copy(bf16[5,10,5,128,128]{4,3,2,1,0:T(8,128)(2,1)} %bitcast.50) | data formatting | bytes 16384000 | tf_op jit(solution)/shard_map/while/body/eval_jaxpr/gather | solution.py:64
  537.9 6.1 fusion.31
  544.0 1.8 copy.66
  545.8 1.3 constant_dynamic-update-slice_fusion.2
  547.1 0.9 fusion.30
  548.1 17.9 %gather_fusion = bf16[250,128,128]{2,1,0:T(8,128)(2,1)} fusion(bf16[100,5,128,128]{3,2,1,0:T(8,128)(2,1)} %get-tuple-element.159, s32[250]{0:T(256)S(1)} %reshape.174), kind=kCustom, calls=%fused_computation.clone.1 | custom fusion | bytes 16386000 | tf_op jit(solution)/shard_map/while/body/eval_jaxpr/gather | solution.py:64
  566.0 12.8 %copy.65 = bf16[5,10,5,128,128]{3,4,1,2,0:T(8,128)(2,1)} copy(bf16[5,10,5,128,128]{4,3,2,1,0:T(8,128)(2,1)} %bitcast.50) | data formatting | bytes 16384000 | tf_op jit(solution)/shard_map/while/body/eval_jaxpr/gather | solution.py:64
  578.9 6.1 fusion.31
  584.9 1.8 copy.66
  586.7 1.3 constant_dynamic-update-slice_fusion.2
  588.0 0.9 fusion.30
  589.0 17.9 %gather_fusion = bf16[250,128,128]{2,1,0:T(8,128)(2,1)} fusion(bf16[100,5,128,128]{3,2,1,0:T(8,128)(2,1)} %get-tuple-element.159, s32[250]{0:T(256)S(1)} %reshape.174), kind=kCustom, calls=%fused_computation.clone.1 | custom fusion | bytes 16386000 | tf_op jit(solution)/shard_map/while/body/eval_jaxpr/gather | solution.py:64
  606.9 12.8 %copy.65 = bf16[5,10,5,128,128]{3,4,1,2,0:T(8,128)(2,1)} copy(bf16[5,10,5,128,128]{4,3,2,1,0:T(8,128)(2,1)} %bitcast.50) | data formatting | bytes 16384000 | tf_op jit(solution)/shard_map/while/body/eval_jaxpr/gather | solution.py:64
  619.8 6.1 fusion.31
  625.9 1.8 copy.66
  627.7 1.3 constant_dynamic-update-slice_fusion.2
  628.9 0.9 fusion.30
  629.9 17.9 %gather_fusion = bf16[250,128,128]{2,1,0:T(8,128)(2,1)} fusion(bf16[100,5,128,128]{3,2,1,0:T(8,128)(2,1)} %get-tuple-element.159, s32[250]{0:T(256)S(1)} %reshape.174), kind=kCustom, calls=%fused_computation.clone.1 | custom fusion | bytes 16386000 | tf_op jit(solution)/shard_map/while/body/eval_jaxpr/gather | solution.py:64
  647.9 12.8 %copy.65 = bf16[5,10,5,128,128]{3,4,1,2,0:T(8,128)(2,1)} copy(bf16[5,10,5,128,128]{4,3,2,1,0:T(8,128)(2,1)} %bitcast.50) | data formatting | bytes 16384000 | tf_op jit(solution)/shard_map/while/body/eval_jaxpr/gather | solution.py:64
  660.7 6.1 fusion.31
  666.8 1.8 copy.66
  668.6 1.3 constant_dynamic-update-slice_fusion.2
  669.9 0.9 fusion.30
  670.9 17.9 %gather_fusion = bf16[250,128,128]{2,1,0:T(8,128)(2,1)} fusion(bf16[100,5,128,128]{3,2,1,0:T(8,128)(2,1)} %get-tuple-element.159, s32[250]{0:T(256)S(1)} %reshape.174), kind=kCustom, calls=%fused_computation.clone.1 | custom fusion | bytes 16386000 | tf_op jit(solution)/shard_map/while/body/eval_jaxpr/gather | solution.py:64
  688.8 12.8 %copy.65 = bf16[5,10,5,128,128]{3,4,1,2,0:T(8,128)(2,1)} copy(bf16[5,10,5,128,128]{4,3,2,1,0:T(8,128)(2,1)} %bitcast.50) | data formatting | bytes 16384000 | tf_op jit(solution)/shard_map/while/body/eval_jaxpr/gather | solution.py:64
  701.7 6.1 fusion.31
  707.8 1.8 copy.66
  709.5 1.3 constant_dynamic-update-slice_fusion.2
  710.8 0.9 fusion.30
  711.8 17.9 %gather_fusion = bf16[250,128,128]{2,1,0:T(8,128)(2,1)} fusion(bf16[100,5,128,128]{3,2,1,0:T(8,128)(2,1)} %get-tuple-element.159, s32[250]{0:T(256)S(1)} %reshape.174), kind=kCustom, calls=%fused_computation.clone.1 | custom fusion | bytes 16386000 | tf_op jit(solution)/shard_map/while/body/eval_jaxpr/gather | solution.py:64
  729.8 12.8 %copy.65 = bf16[5,10,5,128,128]{3,4,1,2,0:T(8,128)(2,1)} copy(bf16[5,10,5,128,128]{4,3,2,1,0:T(8,128)(2,1)} %bitcast.50) | data formatting | bytes 16384000 | tf_op jit(solution)/shard_map/while/body/eval_jaxpr/gather | solution.py:64
  742.6 6.1 fusion.31
  748.7 1.8 copy.66
  750.5 1.4 constant_dynamic-update-slice_fusion.2
  751.9 0.6 copy-done.1
  752.6 256.4 %reduce-scatter.2.cloned.1.call-done = f32[5,5,128,128]{3,2,1,0:T(8,128)} async-done(((f32[40,5,128,128]{3,2,1,0:T(8,128)}), f32[5,5,128,128]{3,2,1,0:T(8,128)}) %reduce-scatter.2.cloned.1.call-update) | async-done | bytes 1638416 | tf_op jit(solution)/shard_map/reduce_scatter | solution.py:80
  1009.0 2.9 fusion.18
  (54 shorter events, 2.8 us)
Async XLA Ops:
  12.2 96.9 %all-to-all-start = ((bf16[8,5,5,128,128]{4,3,2,1,0:T(8,128)(2,1)}), bf16[8,5,5,128,128]{4,3,2,1,0:T(8,128)(2,1)}, u32[]{:S(2)}, u32[]{:S(2)}) async-start(bf16[8,5,5,128,128]{4,3,2,1,0:T(8,128)(2,1)} %stack.2), calls=%async_computation | async-start | bytes 13107200 | tf_op jit(solution)/shard_map/all_to_all | solution.py:30
  18.5 395.7 %all-reduce.4.cloned.1.call-start = ((), (), s32[]{:S(2)}) async-start(), calls=%async_computation.3 | async-start | bytes 26214400 | tf_op jit(solution)/shard_map/psum | solution.py:11
  117.4 0.7 copy-start
  117.5 891.5 %reduce-scatter.2.cloned.1.call-start = ((), (), s32[]{:S(2)}) async-start(), calls=%async_computation.2 | async-start | bytes 14745600 | tf_op jit(solution)/shard_map/reduce_scatter | solution.py:80
  751.8 0.7 copy-start.1
Sparse Core Ops, SparseCore 0:
  117.6 296.5 all-reduce.3
  752.0 256.9 reduce-scatter.1
